TPU v7x, 256 devices: a whole 4x4x8 slice. The times are simulated.
256 devices in a mesh: rows: 64 (over z, y, core), cols: 4 (over x).
Axes of the slice: x: 4, y: 4, z: 8, core: 2. Of those that a mesh axis runs over, the one named last changes fastest.
Arguments:
- crawl: bfloat16 [65536, 128], P('rows'), may hold values from -16 to 16
- bench: bfloat16 [16384, 128], P('cols'), may hold values from -2 to 2
- start_duals: float32 [16384], P('cols'), may hold values from -0.15 to 0.15
- row_cotangent: float32 [65536], P('rows'), may hold values from -24 to 24
- col_cotangent: float32 [16384], P('cols'), may hold values from -24 to 24
Outputs:
- crawl_grad: float32 [65536, 128], P('rows')
- bench_grad: float32 [16384, 128], P('cols')
All inputs are finite; a program needn't handle non-finite values.
Results may differ from a plain program's by a relative error of at most 0.0039.
Values sent between devices are 32-bit elements; how exact they have to be, the bound alone decides.
A program may use at most 64 MiB of HBM per device.

v0:
```python
import math

import jax
import jax.numpy as jnp
from jax import lax
from jax.sharding import PartitionSpec as P

EPSILON = 0.05


def row_lse(logits):
    highest = jnp.max(logits, 1)
    highest = lax.pmax(highest, "cols")
    summed = lax.psum(jnp.sum(jnp.exp(logits - highest[:, None]), 1), "cols")
    return highest + jnp.log(summed)


def col_lse(logits):
    highest = jnp.max(logits, 0)
    highest = lax.pmax(highest, "rows")
    summed = lax.psum(jnp.sum(jnp.exp(logits - highest[None, :]), 0), "rows")
    return highest + jnp.log(summed)


def row_reduce(values):
    return lax.psum(jnp.sum(values, 1), "cols")


def per_device(crawl, bench, start_duals, row_cotangent, col_cotangent):
    log_bench = math.log(bench.shape[0] * lax.axis_size("cols"))
    log_crawl = math.log(crawl.shape[0] * lax.axis_size("rows"))
    tile = lax.dot_general(
        crawl, bench, (((1,), (1,)), ((), ())), preferred_element_type=jnp.float32
    )
    row_level1 = row_lse((start_duals[None, :] + tile) / EPSILON)
    row_dual1 = -EPSILON * (row_level1 - log_bench)
    col_level1 = col_lse((row_dual1[:, None] + tile) / EPSILON)
    col_dual1 = -EPSILON * (col_level1 - log_crawl)
    row_level2 = row_lse((col_dual1[None, :] + tile) / EPSILON)
    row_dual2 = -EPSILON * (row_level2 - log_bench)
    col_level2 = col_lse((row_dual2[:, None] + tile) / EPSILON)
    col_soft2 = jnp.exp((row_dual2[:, None] + tile) / EPSILON - col_level2[None, :])
    row_back2 = row_cotangent - row_reduce(col_soft2 * col_cotangent[None, :])
    row_soft2 = jnp.exp((col_dual1[None, :] + tile) / EPSILON - row_level2[:, None])
    col_back1 = -lax.psum(jnp.sum(row_soft2 * row_back2[:, None], 0), "rows")
    col_soft1 = jnp.exp((row_dual1[:, None] + tile) / EPSILON - col_level1[None, :])
    row_back1 = -row_reduce(col_soft1 * col_back1[None, :])
    row_soft1 = jnp.exp((start_duals[None, :] + tile) / EPSILON - row_level1[:, None])
    score_grad = -(
        col_soft2 * col_cotangent[None, :]
        + row_soft2 * row_back2[:, None]
        + col_soft1 * col_back1[None, :]
        + row_soft1 * row_back1[:, None]
    )
    score_grad = score_grad.astype(jnp.bfloat16)
    crawl_part = jnp.dot(score_grad, bench, preferred_element_type=jnp.float32)
    crawl_grad = lax.psum(crawl_part, "cols")
    bench_part = lax.dot_general(
        score_grad, crawl, (((0,), (0,)), ((), ())), preferred_element_type=jnp.float32
    )
    bench_grad = lax.psum(bench_part, "rows")
    return (crawl_grad, bench_grad)


def solution(mesh):
    placed = (P("rows", None), P("cols", None), P("cols"), P("rows"), P("cols"))
    return jax.shard_map(
        per_device,
        mesh=mesh,
        in_specs=placed,
        out_specs=(P("rows", None), P("cols", None)),
        check_vma=False,
    )
```

profile of v0, /device:TPU:1, one launch (start us, length us, event | category | flops | bytes accessed | tf_op | source)
XLA Modules:
  0.0 1658.6 jit_solution(8638071974388296962)
XLA Ops:
  8.4 7.9 fusion.3
  16.3 9.3 pmax.28
  25.6 7.8 exponential_reduce_fusion.3
  33.4 6.0 psum.63
  39.5 7.7 fusion.4
  47.2 248.9 %pmax.29 = f32[4096]{0:T(1024)S(1)} all-reduce(f32[4096]{0:T(1024)S(1)} %fusion.4), channel_id=1, replica_groups=mesh['rows'=64,'cols'=4] {'rows'}, use_global_device_ids=true, to_apply=%region_5.0 | all-reduce | flops 4096 | bytes 32768 | tf_op jit(solution)/shard_map/pmax | solution.py:20
  296.1 7.7 exponential_reduce_fusion.2
  303.8 246.1 %psum.64 = f32[4096]{0:T(1024)S(1)} all-reduce(f32[4096]{0:T(1024)S(1)} %exponential_reduce_fusion.2), channel_id=1, replica_groups=mesh['rows'=64,'cols'=4] {'rows'}, use_global_device_ids=true, to_apply=%region_7.0 | all-reduce | flops 4096 | bytes 32768 | tf_op jit(solution)/shard_map/psum | solution.py:21
  550.0 7.5 fusion.5
  557.5 7.7 pmax.30
  565.2 7.8 exponential_reduce_fusion.1
  579.1 7.7 fusion.6
  586.8 250.1 %pmax.31 = f32[4096]{0:T(1024)S(1)} all-reduce(f32[4096]{0:T(1024)S(1)} %fusion.6), channel_id=1, replica_groups=mesh['rows'=64,'cols'=4] {'rows'}, use_global_device_ids=true, to_apply=%region_13.0 | all-reduce | flops 4096 | bytes 32768 | tf_op jit(solution)/shard_map/pmax | solution.py:20
  836.9 7.7 exponential_reduce_fusion
  844.6 246.1 %psum.66 = f32[4096]{0:T(1024)S(1)} all-reduce(f32[4096]{0:T(1024)S(1)} %exponential_reduce_fusion), channel_id=1, replica_groups=mesh['rows'=64,'cols'=4] {'rows'}, use_global_device_ids=true, to_apply=%region_15.0 | all-reduce | flops 4096 | bytes 32768 | tf_op jit(solution)/shard_map/psum | solution.py:21
  1090.8 8.2 fusion
  1099.0 7.7 psum.67
  1106.7 8.1 fusion.1
  1114.9 248.2 %psum.68 = f32[4096]{0:T(1024)S(1)} all-reduce(f32[4096]{0:T(1024)S(1)} %fusion.1), channel_id=1, replica_groups=mesh['rows'=64,'cols'=4] {'rows'}, use_global_device_ids=true, to_apply=%region_19.0 | all-reduce | flops 4096 | bytes 32768 | tf_op jit(solution)/shard_map/psum | solution.py:45
  1363.0 8.1 fusion.2
  1377.2 20.0 %negate_convert_fusion = bf16[1024,4096]{1,0:T(8,128)(2,1)S(1)} fusion(f32[1024,4096]{1,0:T(8,128)} %get-tuple-element.9, f32[1024]{0:T(1024)S(1)} %neg.10, f32[1024]{0:T(1024)S(1)} %get-tuple-element.7, f32[4096]{0:T(1024)S(1)} %neg.9, f32[4096]{0:T(1024)S(1)} %get-tuple-element.5, f32[1024]{0:T(1024)S(1)} %sub.92, f32[1024]{0:T(1024)S(1)} %get-tuple-element.3, ...), kind=kLoop, calls=%fused_computation | loop fusion | flops 88080384 | bytes 25288704 | tf_op jit(solution)/shard_map/convert_element_type | solution.py:55
  1403.8 7.1 fusion.8
  1411.0 41.3 %all-reduce.3.cloned.1.call-done = f32[1024,128]{1,0:T(8,128)} async-done(((f32[1024,128]{1,0:T(8,128)}), f32[1024,128]{1,0:T(8,128)}) %all-reduce.3.cloned.1.call-update) | async-done | bytes 524304 | tf_op jit(solution)/shard_map/psum | solution.py:57
  1452.3 194.6 %all-reduce.5.cloned.1.call-done = f32[4096,128]{1,0:T(8,128)} async-done(((f32[4096,128]{1,0:T(8,128)}), f32[4096,128]{1,0:T(8,128)}) %all-reduce.5.cloned.1.call-update) | async-done | bytes 2097168 | tf_op jit(solution)/shard_map/psum | solution.py:61
  (28 shorter events, 24.8 us)
Async XLA Ops:
  7.2 1.2 copy-start
  7.2 18.4 %copy-start.3 = (f32[4096]{0:T(1024)S(1)}, f32[4096]{0:T(1024)}, u32[]{:S(2)}) copy-start(f32[4096]{0:T(1024)} %param.7) | copy-start | bytes 49156
  7.2 1445.1 %all-reduce.3.cloned.1.call-start = ((), (), s32[]{:S(2)}) async-start(), calls=%async_computation | async-start | bytes 1048576 | tf_op jit(solution)/shard_map/psum | solution.py:57
  579.1 511.7 %copy-start.4 = (f32[4096]{0:T(1024)S(1)}, f32[4096]{0:T(1024)}, u32[]{:S(2)}) copy-start(f32[4096]{0:T(1024)} %param.9) | copy-start | bytes 49156
  836.9 269.9 %copy-start.5 = (f32[1024]{0:T(1024)S(1)}, f32[1024]{0:T(1024)}, u32[]{:S(2)}) copy-start(f32[1024]{0:T(1024)} %param.8) | copy-start | bytes 12292
  1377.2 26.7 %copy-start.2 = (bf16[1024,128]{1,0:T(8,128)(2,1)S(1)}, bf16[1024,128]{1,0:T(8,128)(2,1)}, u32[]{:S(2)}) copy-start(bf16[1024,128]{1,0:T(8,128)(2,1)} %param.5) | copy-start | bytes 786436
  1397.2 3.2 copy-start.1
  1403.6 243.3 %all-reduce.5.cloned.1.call-start = ((), (), s32[]{:S(2)}) async-start(), calls=%async_computation.1 | async-start | bytes 4194304 | tf_op jit(solution)/shard_map/psum | solution.py:61
Sparse Core Ops, SparseCore 0:
  1403.7 48.5 all-reduce.2
  1456.3 190.5 all-reduce.4
where the time goes:
time: 1660 us
  blocking collectives  1280 us (77%)
  waiting for transfers between devices  236 us (14%)
  other arithmetic  98.6 us (6%)
  matrix products  18.2 us (1%)
    pmax x2, blocking collectives, col_lse(): highest = lax.pmax(highest, 'rows')  499 us
    psum x2, blocking collectives, col_lse(): summed = lax.psum(jnp.sum(jnp.exp(logits - highest[None, :]), 0), 'rows')  492 us
    psum x1, blocking collectives, per_device(): col_back1 = -lax.psum(jnp.sum(row_soft2 * row_back2[:, None], 0), 'rows')  248 us
    psum x1, waiting for transfers between devices, per_device(): bench_grad = lax.psum(bench_part, 'rows')  195 us
    psum x1, waiting for transfers between devices, per_device(): crawl_grad = lax.psum(crawl_part, 'cols')  41.3 us
  transfers between devices with their start and end apart: 2, of which 2 were waited for; matrix products, arithmetic and copies ran while one was open for 0% of the time, Pallas kernels for 0%

commit v1 on v0

v1 whole, which is shorter than its diff:
```python
import functools
import math

import jax
import jax.numpy as jnp
from jax import lax
from jax.experimental import pallas as pl
from jax.experimental.pallas import tpu as pltpu
from jax.sharding import PartitionSpec as P

EPSILON = 0.05
SCALE = math.log2(math.e) / EPSILON
MESH = pl.DeviceIdType.MESH
F32 = jnp.float32
CORES, YS = 2, 4


def kernel(
    nx, nz,
    crawl, bench, start, row_cot, col_cot,
    crawl_out, bench_out,
    tile, crawl_t, grads, lane_max, lane_sum, alpha_b, beta_b, back_b,
    rowvec, colmax, fvec, gvec, avec, bvec,
    xs1, xr1, xs, xr, as1, ar1, as_, ar, zs1, zr1, zs, zr, cg,
    crawl_acc, crawl_recv, bench_part, sib, ysend, yrecv, zpart, zrecv,
    x_ss, x_rs, a_ss, a_rs, z_ss, z_rs, g_ss, g_rs,
    cr_ss, cr_rs, ca_ss, ca_rs, sib_ss, sib_rs, y_ss, y_rs, fz_ss, fz_rs,
    gz_ss, gz_rs, gy_ss, gy_rs, gc_ss, gc_rs,
):
    rows, depth = crawl.shape
    cols = bench.shape[0]
    half, part = cols // CORES, cols // (CORES * YS)
    na = CORES * YS
    r, c = lax.axis_index("rows"), lax.axis_index("cols")
    k, y, z = lax.rem(r, CORES), lax.rem(lax.div(r, CORES), YS), lax.div(r, na)
    a = lax.rem(r, na)

    def at(k_, y_, z_):
        return ((z_ * YS + y_) * CORES + k_, c)

    x_peers = [(r, lax.rem(c + d, nx)) for d in range(1, nx)]
    a_peers = []
    for d in range(1, na):
        o = lax.rem(a + d, na)
        a_peers.append((lax.rem(o, CORES), at(lax.rem(o, CORES), lax.div(o, CORES), z)))
    z_peers = [(lax.rem(z + d, nz), at(k, y, lax.rem(z + d, nz))) for d in range(1, nz)]
    sibling = at(1 - k, y, z)

    barrier = pltpu.get_barrier_semaphore()
    everyone = x_peers + [p for _, p in a_peers] + [p for _, p in z_peers]
    for p in everyone:
        pl.semaphore_signal(barrier, inc=1, device_id=p, device_id_type=MESH)

    def send(src, dst, ss, rs, p):
        pltpu.make_async_remote_copy(
            src_ref=src, dst_ref=dst, send_sem=ss, recv_sem=rs, device_id=p, device_id_type=MESH
        ).start()

    def take(ref, sem):
        pltpu.make_async_copy(ref, ref, sem).wait()

    def x_exchange(n, src, recv):
        recv[c] = src[...]
        for p in x_peers:
            send(src, recv.at[c], x_ss.at[n], x_rs.at[n], p)
        others = recv.at[pl.ds(0, nx - 1)]
        take(others, x_rs.at[n])
        take(others, x_ss.at[n])

    def a_exchange(n, src, recv):
        recv[a] = src[k]
        for o, p in a_peers:
            send(src.at[o], recv.at[a], a_ss.at[n], a_rs.at[n], p)
        others = recv.at[pl.ds(0, na - 1)]
        take(others, a_rs.at[n])
        take(others, a_ss.at[n])

    def z_exchange(n, src, recv):
        recv[z] = src[...]
        for _, p in z_peers:
            send(src, recv.at[z], z_ss.at[n], z_rs.at[n], p)
        others = recv.at[pl.ds(0, nz - 1)]
        take(others, z_rs.at[n])
        take(others, z_ss.at[n])

    def core_gather(n, value):
        cg[n, k] = value
        send(cg.at[n, k], cg.at[n, k], g_ss.at[n], g_rs.at[n], sibling)
        take(cg.at[n, k], g_rs.at[n])
        take(cg.at[n, k], g_ss.at[n])

    def summed(recv, n):
        total = recv[0]
        for i in range(1, n):
            total = total + recv[i]
        return total

    def combined(recv, n):
        top = recv[0, 0:1, :]
        for i in range(1, n):
            top = jnp.maximum(top, recv[i, 0:1, :])
        total = recv[0, 1:2, :] * jnp.exp2(recv[0, 0:1, :] - top)
        for i in range(1, n):
            total = total + recv[i, 1:2, :] * jnp.exp2(recv[i, 0:1, :] - top)
        return top, total

    def spread(vec, out):
        for i in range(rows // 128):
            piece = vec[:, i * 128 : (i + 1) * 128]
            out[i * 128 : (i + 1) * 128, :] = jnp.broadcast_to(piece, (128, 128)).T

    def row_pass(d, out):
        def step(i, carry):
            base = pl.multiple_of(i * 128, 128)
            pieces = []
            for h in range(2):
                acc = jnp.zeros((64, 128), F32)
                for j in range(cols // 128):
                    s = slice(j * 128, (j + 1) * 128)
                    acc = acc + tile[pl.ds(base + h * 64, 64), s] * d[0:1, s]
                pieces.append(acc)
            acc = jnp.concatenate(pieces, 0).T
            out[0:1, pl.ds(base, 128)] = jnp.sum(acc, 0, keepdims=True)
            return carry

        lax.fori_loop(0, rows // 128, step, 0)

    width = min(1024, cols)

    def col_pass(w, finish):
        for cb in range(cols // width):
            def step(i, accs, cb=cb):
                base = pl.multiple_of(i * 64, 64)
                wb = w[pl.ds(base, 64), :]
                new = []
                for j in range(width // 128):
                    o = cb * width + j * 128
                    t = tile[pl.ds(base, 64), o : o + 128] * wb
                    new.append(accs[j] + jnp.sum(t.reshape(8, 8, 128), 0))
                return tuple(new)

            accs = lax.fori_loop(
                0, rows // 64, step, tuple(jnp.zeros((8, 128), F32) for _ in range(width // 128))
            )
            for j in range(width // 128):
                finish(cb * width + j * 128, jnp.sum(accs[j], 0, keepdims=True))

    crawl_t[...] = crawl[...].astype(F32).T.astype(jnp.bfloat16)
    lane_max[...] = jnp.full(lane_max.shape, -jnp.inf, F32)
    mm = min(512, cols)
    rb = min(256, rows)

    def score_step(t, carry):
        i, jb = lax.rem(t, rows // rb), lax.div(t, rows // rb)
        base = pl.multiple_of(i * rb, rb)
        off = pl.multiple_of(jb * mm, mm)
        s = lax.dot_general(
            crawl[pl.ds(base, rb), :], bench[pl.ds(off, mm), :], (((1,), (1,)), ((), ())),
            preferred_element_type=F32,
        )
        s = s * SCALE + start[0:1, pl.ds(off, mm)] * SCALE
        tile[pl.ds(base, rb), pl.ds(off, mm)] = s
        top = lane_max[pl.ds(base, rb), :]
        for j in range(mm // 128):
            top = jnp.maximum(top, s[:, j * 128 : (j + 1) * 128])
        lane_max[pl.ds(base, rb), :] = top
        return carry

    lax.fori_loop(0, (rows // rb) * (cols // mm), score_step, 0)

    def level_step(i, carry):
        base = pl.multiple_of(i * 128, 128)
        tops, sums = [], []
        for h in range(2):
            at_ = pl.ds(base + h * 64, 64)
            top = lane_max[at_, :]
            acc = jnp.zeros((64, 128), F32)
            for j in range(cols // 128):
                acc = acc + jnp.exp2(tile[at_, j * 128 : (j + 1) * 128] - top)
            tops.append(top)
            sums.append(acc)
        top = jnp.concatenate(tops, 0).T
        acc = jnp.concatenate(sums, 0).T
        best = jnp.max(top, 0, keepdims=True)
        xs1[0:1, pl.ds(base, 128)] = best
        xs1[1:2, pl.ds(base, 128)] = jnp.sum(acc * jnp.exp2(top - best), 0, keepdims=True)
        return carry

    lax.fori_loop(0, rows // 128, level_step, 0)
    pl.semaphore_wait(barrier, len(everyone))
    x_exchange(0, xs1, xr1)
    top, total = combined(xr1, nx)
    spread(top + jnp.log2(total), alpha_b)

    for cb in range(cols // width):
        def top_step(i, tops, cb=cb):
            base = pl.multiple_of(i * 64, 64)
            lev = alpha_b[pl.ds(base, 64), :]
            new = []
            for j in range(width // 128):
                o = cb * width + j * 128
                t = tile[pl.ds(base, 64), o : o + 128] - lev
                new.append(jnp.maximum(tops[j], jnp.max(t.reshape(8, 8, 128), 0)))
            return tuple(new)

        tops = lax.fori_loop(
            0, rows // 64, top_step, tuple(jnp.full((8, 128), -jnp.inf, F32) for _ in range(width // 128))
        )
        tops = [jnp.max(t, 0, keepdims=True) for t in tops]
        for j in range(width // 128):
            colmax[0:1, cb * width + j * 128 : cb * width + (j + 1) * 128] = tops[j]

        def exp_step(i, accs, cb=cb):
            base = pl.multiple_of(i * 64, 64)
            lev = alpha_b[pl.ds(base, 64), :]
            new = []
            for j in range(width // 128):
                o = cb * width + j * 128
                e = jnp.exp2((tile[pl.ds(base, 64), o : o + 128] - lev) - colmax[0:1, o : o + 128])
                tile[pl.ds(base, 64), o : o + 128] = e
                new.append(accs[j] + jnp.sum(e.reshape(8, 8, 128), 0))
            return tuple(new)

        accs = lax.fori_loop(
            0, rows // 64, exp_step, tuple(jnp.zeros((8, 128), F32) for _ in range(width // 128))
        )
        for j in range(width // 128):
            o = cb * width + j * 128
            h, p = o // half, o % half
            as1[h, 0:1, p : p + 128] = tops[j]
            as1[h, 1:2, p : p + 128] = jnp.sum(accs[j], 0, keepdims=True)
    gvec[...] = jnp.exp2(colmax[...])

    a_exchange(0, as1, ar1)
    top, total = combined(ar1, na)
    zs1[0:1, :] = top
    zs1[1:2, :] = total
    z_exchange(0, zs1, zr1)
    top, total = combined(zr1, nz)
    core_gather(0, top + jnp.log2(total))
    for h in range(CORES):
        s = slice(h * half, (h + 1) * half)
        fvec[0:1, s] = jnp.exp2(colmax[0:1, s] - cg[0, h])

    row_pass(fvec, xs.at[0])
    x_exchange(1, xs.at[0], xr.at[0])
    alpha = 1.0 / summed(xr.at[0], nx)
    rowvec[...] = alpha
    spread(alpha, alpha_b)

    def col_reduce(n, w):
        def finish(o, v):
            h, p = o // half, o % half
            as_[n, h, 0:1, p : p + 128] = v * fvec[0:1, o : o + 128]

        col_pass(w, finish)
        a_exchange(n + 1, as_.at[n], ar.at[n])
        zs[n] = summed(ar.at[n], na)
        z_exchange(n + 1, zs.at[n], zr.at[n])
        core_gather(n + 1, summed(zr.at[n], nz))

    col_reduce(0, alpha_b)
    for h in range(CORES):
        s = slice(h * half, (h + 1) * half)
        avec[0:1, s] = fvec[0:1, s] * col_cot[0:1, s] / cg[1, h]

    row_pass(avec, xs.at[1])
    x_exchange(2, xs.at[1], xr.at[1])
    back2 = row_cot[...] - rowvec[...] * summed(xr.at[1], nx)
    spread(back2 * rowvec[...], beta_b)

    col_reduce(1, beta_b)
    for h in range(CORES):
        s = slice(h * half, (h + 1) * half)
        bvec[0:1, s] = -fvec[0:1, s] * cg[2, h]

    row_pass(bvec, xs.at[2])
    x_exchange(3, xs.at[2], xr.at[2])
    spread(-summed(xr.at[2], nx), back_b)

    crawl_acc[...] = jnp.zeros(crawl_acc.shape, F32)

    def grad_chunk(off, out):
        def step(i, carry):
            base = pl.multiple_of(i * 64, 64)
            al, be, ba = (v[pl.ds(base, 64), :] for v in (alpha_b, beta_b, back_b))
            for j in range(part // 128):
                s = pl.ds(pl.multiple_of(off + j * 128, 128), 128)
                bracket = (al * avec[0:1, s] + be * fvec[0:1, s]) + (bvec[0:1, s] + ba * gvec[0:1, s])
                value = -(tile[pl.ds(base, 64), s] * bracket)
                grads[pl.ds(base, 64), j * 128 : (j + 1) * 128] = value.astype(jnp.bfloat16)
            return carry

        lax.fori_loop(0, rows // 64, step, 0)

        def product(i, carry):
            base = pl.multiple_of(i * rb, rb)
            crawl_acc[pl.ds(base, rb), :] += jnp.dot(
                grads[pl.ds(base, rb), :], bench[pl.ds(off, part), :], preferred_element_type=F32
            )
            return carry

        lax.fori_loop(0, rows // rb, product, 0)
        out[...] = jnp.dot(crawl_t[...], grads[...], preferred_element_type=F32)

    def ordered(s):
        return lax.rem(y + (2, 1, 3, 0)[s], YS)

    for s in range(YS):
        owner = ordered(s)
        theirs = pl.multiple_of((1 - k) * half + owner * part, part)
        mine = pl.multiple_of(k * half + owner * part, part)
        grad_chunk(theirs, bench_part.at[s])
        send(bench_part.at[s], sib.at[s], sib_ss.at[s], sib_rs.at[s], sibling)
        grad_chunk(mine, ysend.at[s])
        take(sib.at[s], sib_rs.at[s])
        if s < YS - 1:
            ysend[s] = ysend[s] + sib[s]
            send(ysend.at[s], yrecv.at[y], y_ss.at[s], y_rs, at(k, owner, z))
        else:
            yrecv[y] = ysend[s] + sib[s]

    quarter = rows // nx
    mine_rows = pl.ds(pl.multiple_of(c * quarter, quarter), quarter)
    for d, p in enumerate(x_peers):
        there = pl.ds(pl.multiple_of(p[1] * quarter, quarter), quarter)
        send(crawl_acc.at[there, :], crawl_recv.at[c], cr_ss.at[d], cr_rs, p)
    crawl_recv[c] = crawl_acc[mine_rows, :]

    others = yrecv.at[pl.ds(0, YS - 1)]
    take(others, y_rs)
    piece = part // nz
    for j in range(part // 128):
        s = slice(j * 128, (j + 1) * 128)
        total = yrecv[0, :, s]
        for i in range(1, YS):
            total = total + yrecv[i, :, s]
        zpart[s, :] = total.T
    for d, (o, p) in enumerate(z_peers):
        send(zpart.at[pl.ds(pl.multiple_of(o * piece, piece), piece), :], zrecv.at[z], fz_ss.at[d], fz_rs, p)
    zrecv[z] = zpart[pl.ds(pl.multiple_of(z * piece, piece), piece), :]

    take(crawl_recv.at[pl.ds(0, nx - 1)], cr_rs)
    crawl_out[mine_rows, :] = summed(crawl_recv, nx)
    for d, p in enumerate(x_peers):
        send(crawl_out.at[mine_rows, :], crawl_out.at[mine_rows, :], ca_ss.at[d], ca_rs, p)

    take(zrecv.at[pl.ds(0, nz - 1)], fz_rs)
    block = pl.multiple_of(k * half + y * part, part)
    own = pl.ds(pl.multiple_of(block + z * piece, piece), piece)
    bench_out[own, :] = summed(zrecv, nz)
    for d, (_, p) in enumerate(z_peers):
        send(bench_out.at[own, :], bench_out.at[own, :], gz_ss.at[d], gz_rs, p)
    take(zrecv.at[pl.ds(0, nz - 1)], gz_rs)
    mine_block = pl.ds(block, part)
    for s in range(YS - 1):
        send(bench_out.at[mine_block, :], bench_out.at[mine_block, :], gy_ss.at[s], gy_rs.at[s], at(k, ordered(s), z))
    send(bench_out.at[mine_block, :], bench_out.at[mine_block, :], gc_ss.at[YS - 1], gc_rs.at[YS - 1], sibling)
    for s in range(YS - 1):
        source = lax.rem(y + YS - (2, 1, 3)[s], YS)
        theirs = pl.ds(pl.multiple_of(k * half + source * part, part), part)
        take(bench_out.at[theirs, :], gy_rs.at[s])
        send(bench_out.at[theirs, :], bench_out.at[theirs, :], gc_ss.at[s], gc_rs.at[s], sibling)
    for s in range(YS):
        take(sib.at[s], gc_rs.at[s])
        take(sib.at[s], gc_ss.at[s])
        take(sib.at[s], sib_ss.at[s])
    for s in range(YS - 1):
        take(sib.at[s], gy_ss.at[s])
        take(sib.at[s], y_ss.at[s])
    for d in range(nz - 1):
        take(zrecv.at[0], fz_ss.at[d])
        take(zrecv.at[0], gz_ss.at[d])
    take(crawl_recv.at[pl.ds(0, nx - 1)], ca_rs)
    for d in range(nx - 1):
        take(crawl_recv.at[0], ca_ss.at[d])
        take(crawl_recv.at[0], cr_ss.at[d])


def solution(mesh):
    nx = mesh.shape["cols"]
    nz = mesh.shape["rows"] // (CORES * YS)
    na = CORES * YS

    def per_device(crawl, bench, start_duals, row_cotangent, col_cotangent):
        rows, depth = crawl.shape
        cols = bench.shape[0]
        half, part = cols // CORES, cols // (CORES * YS)
        vmem, dma = pltpu.VMEM, pltpu.SemaphoreType.DMA
        scratch = [
            vmem((rows, cols), F32),
            vmem((depth, rows), jnp.bfloat16),
            vmem((rows, part), jnp.bfloat16),
            vmem((rows, 128), F32),
            vmem((rows, 128), F32),
            vmem((rows, 128), F32),
            vmem((rows, 128), F32),
            vmem((rows, 128), F32),
            vmem((1, rows), F32),
            *[vmem((1, cols), F32)] * 5,
            vmem((2, rows), F32), vmem((nx, 2, rows), F32),
            vmem((3, 1, rows), F32), vmem((3, nx, 1, rows), F32),
            vmem((CORES, 2, half), F32), vmem((na, 2, half), F32),
            vmem((2, CORES, 1, half), F32), vmem((2, na, 1, half), F32),
            vmem((2, half), F32), vmem((nz, 2, half), F32),
            vmem((2, 1, half), F32), vmem((2, nz, 1, half), F32),
            vmem((3, CORES, 1, half), F32),
            vmem((rows, depth), F32), vmem((nx, rows // nx, depth), F32),
            vmem((YS, depth, part), F32), vmem((YS, depth, part), F32),
            vmem((YS, depth, part), F32), vmem((YS, depth, part), F32),
            vmem((part, depth), F32), vmem((nz, part // nz, depth), F32),
            dma((4,)), dma((4,)), dma((3,)), dma((3,)), dma((3,)), dma((3,)), dma((3,)), dma((3,)),
            dma((nx - 1,)), dma, dma((nx - 1,)), dma,
            dma((YS,)), dma((YS,)), dma((YS - 1,)), dma, dma((nz - 1,)), dma,
            dma((nz - 1,)), dma, dma((YS - 1,)), dma((YS - 1,)), dma((YS,)), dma((YS,)),
        ]
        return pl.pallas_call(
            functools.partial(kernel, nx, nz),
            out_shape=(jax.ShapeDtypeStruct((rows, depth), F32), jax.ShapeDtypeStruct((cols, depth), F32)),
            in_specs=[pl.BlockSpec(memory_space=vmem)] * 5,
            out_specs=(pl.BlockSpec(memory_space=vmem),) * 2,
            scratch_shapes=scratch,
            compiler_params=pltpu.CompilerParams(
                collective_id=0, has_side_effects=True, vmem_limit_bytes=56 << 20
            ),
        )(crawl, bench, start_duals[None, :], row_cotangent[None, :], col_cotangent[None, :])

    placed = (P("rows", None), P("cols", None), P("cols"), P("rows"), P("cols"))
    return jax.shard_map(
        per_device,
        mesh=mesh,
        in_specs=placed,
        out_specs=(P("rows", None), P("cols", None)),
        check_vma=False,
    )
```

time: 1660 us -> 133 us (0.08)
  blocking collectives: 1280 us -> 0 us
  waiting for transfers between devices: 236 us -> 0 us
  Pallas kernels: 0 us -> 126 us
  other arithmetic: 98.6 us -> 0 us
  matrix products: 18.2 us -> 0 us
    psum x7 -> x0, blocking collectives: 766 us -> none  [the longest x2 492 us: col_lse(): summed = lax.psum(jnp.sum(jnp.exp(logits - highest[None, :]), 0), 'rows')]
    pmax x4 -> x0, blocking collectives: 516 us -> none  [the longest x2 499 us: col_lse(): highest = lax.pmax(highest, 'rows')]
    psum x2 -> x0, waiting for transfers between devices: 236 us -> none  [the longest x1 195 us: per_device(): bench_grad = lax.psum(bench_part, 'rows')]
    pallas_call x0 -> x1, Pallas kernels: none -> 126 us  [per_device(): pl.pallas_call(functools.partial(kernel, nx, nz), out_shape=(jax.ShapeDty...]
    reduce_sum x7 -> x0, other arithmetic: 55.6 us -> none  [the longest x2 16.3 us: row_reduce(): return lax.psum(jnp.sum(values, 1), 'cols')]
    reduce_max x3 -> x0, other arithmetic: 23 us -> none  [the longest x2 15.5 us: col_lse(): highest = jnp.max(logits, 0)]
    convert_element_type x1 -> x0, other arithmetic: 20 us -> none  [per_device(): score_grad = score_grad.astype(jnp.bfloat16)]
    dot_general x3 -> x0, matrix products: 18.2 us -> none  [the longest x1 7.94 us: per_device(): lax.dot_general(crawl, bench, (((1,), (1,)), ((), ())), preferred_element...]
  transfers between devices with their start and end apart: 2 -> 0, of which waited for: 2 -> 0; matrix products, arithmetic and copies ran while one was open for 0% -> 0% of each run, Pallas kernels for 0% -> 0%
where the time goes in v1:
time: 133 us; the launch traced here: 132 us
  Pallas kernels  126 us (95%)
  local copies, waits for them, and re-layouts  4.91 us (4%)
    pallas_call x1, Pallas kernels, per_device(): pl.pallas_call(functools.partial(kernel, nx, nz), out_shape=(jax.ShapeDty...  126 us
    unnamed x2, local copies, waits for them, and re-layouts  4.91 us

profile of v1, /device:TPU:1, one launch (start us, length us, event | category | flops | bytes accessed | tf_op | source)
XLA Modules:
  0.0 131.6 jit_solution(9677904582147980500)
XLA Ops:
  0.6 126.0 %shard_map.68 = (f32[1024,128]{1,0:T(8,128)}, f32[4096,128]{1,0:T(8,128)}) custom-call(bf16[1024,128]{1,0:T(8,128)(2,1)} %crawl.1, bf16[4096,128]{1,0:T(8,128)(2,1)} %bench.1, f32[1,4096]{1,0:T(1,128)} %bitcast.3, f32[1,1024]{1,0:T(1,128)} %bitcast.5, f32[1,4096]{1,0:T(1,128)} %bitcast.4), custom_call_target="tpu_custom_call" | custom-call | tf_op jit(solution)/shard_map/pallas_call | solution.py:417
  126.7 1.9 %copy.9 = f32[1024,128]{1,0:T(8,128)} copy(f32[1024,128]{1,0:T(8,128)} %get-tuple-element.4) | data formatting | bytes 1048576
  128.5 3.0 %copy.10 = f32[4096,128]{1,0:T(8,128)} copy(f32[4096,128]{1,0:T(8,128)} %get-tuple-element.5) | data formatting | bytes 4194304

commit v2 on v1

--- a/solution.py
+++ b/solution.py
@@ -19,7 +19,7 @@
     nx, nz,
     crawl, bench, start, row_cot, col_cot,
     crawl_out, bench_out,
-    tile, crawl_t, grads, lane_max, lane_sum, alpha_b, beta_b, back_b,
+    tile, crawl_t, lane_max, alpha_b, beta_b, back_b,
     rowvec, colmax, fvec, gvec, avec, bvec,
     xs1, xr1, xs, xr, as1, ar1, as_, ar, zs1, zr1, zs, zr, cg,
     crawl_acc, crawl_recv, bench_part, sib, ysend, yrecv, zpart, zrecv,
@@ -166,7 +166,7 @@
         lane_max[pl.ds(base, rb), :] = top
         return carry
 
-    lax.fori_loop(0, (rows // rb) * (cols // mm), score_step, 0)
+    lax.fori_loop(0, (rows // rb) * (cols // mm), score_step, 0, unroll=4)
 
     def level_step(i, carry):
         base = pl.multiple_of(i * 128, 128)
@@ -280,101 +280,157 @@
 
     crawl_acc[...] = jnp.zeros(crawl_acc.shape, F32)
 
-    def grad_chunk(off, out):
-        def step(i, carry):
-            base = pl.multiple_of(i * 64, 64)
-            al, be, ba = (v[pl.ds(base, 64), :] for v in (alpha_b, beta_b, back_b))
-            for j in range(part // 128):
-                s = pl.ds(pl.multiple_of(off + j * 128, 128), 128)
-                bracket = (al * avec[0:1, s] + be * fvec[0:1, s]) + (bvec[0:1, s] + ba * gvec[0:1, s])
-                value = -(tile[pl.ds(base, 64), s] * bracket)
-                grads[pl.ds(base, 64), j * 128 : (j + 1) * 128] = value.astype(jnp.bfloat16)
-            return carry
-
-        lax.fori_loop(0, rows // 64, step, 0)
-
-        def product(i, carry):
-            base = pl.multiple_of(i * rb, rb)
-            crawl_acc[pl.ds(base, rb), :] += jnp.dot(
-                grads[pl.ds(base, rb), :], bench[pl.ds(off, part), :], preferred_element_type=F32
-            )
-            return carry
-
-        lax.fori_loop(0, rows // rb, product, 0)
-        out[...] = jnp.dot(crawl_t[...], grads[...], preferred_element_type=F32)
-
-    def ordered(s):
-        return lax.rem(y + (2, 1, 3, 0)[s], YS)
-
-    for s in range(YS):
-        owner = ordered(s)
-        theirs = pl.multiple_of((1 - k) * half + owner * part, part)
-        mine = pl.multiple_of(k * half + owner * part, part)
-        grad_chunk(theirs, bench_part.at[s])
-        send(bench_part.at[s], sib.at[s], sib_ss.at[s], sib_rs.at[s], sibling)
-        grad_chunk(mine, ysend.at[s])
-        take(sib.at[s], sib_rs.at[s])
-        if s < YS - 1:
-            ysend[s] = ysend[s] + sib[s]
-            send(ysend.at[s], yrecv.at[y], y_ss.at[s], y_rs, at(k, owner, z))
-        else:
-            yrecv[y] = ysend[s] + sib[s]
-
-    quarter = rows // nx
-    mine_rows = pl.ds(pl.multiple_of(c * quarter, quarter), quarter)
-    for d, p in enumerate(x_peers):
-        there = pl.ds(pl.multiple_of(p[1] * quarter, quarter), quarter)
-        send(crawl_acc.at[there, :], crawl_recv.at[c], cr_ss.at[d], cr_rs, p)
+    def grad_chunk(core, q, out):
+        offs = [pl.multiple_of(core * half + o * part + q * 128, 128) for o in range(YS)]
+        some_bench = jnp.concatenate([bench[pl.ds(o, 128), :] for o in offs], 0)
+        acc = None
+        for i in range(rows // rb):
+            blocks = []
+            for h in range(rb // 64):
+                at_ = slice(i * rb + h * 64, i * rb + (h + 1) * 64)
+                al, be, ba = alpha_b[at_, :], beta_b[at_, :], back_b[at_, :]
+                pieces = []
+                for o in offs:
+                    s = pl.ds(o, 128)
+                    bracket = (al * avec[0:1, s] + be * fvec[0:1, s]) + (bvec[0:1, s] + ba * gvec[0:1, s])
+                    pieces.append((-(tile[at_, s] * bracket)).astype(jnp.bfloat16))
+                blocks.append(jnp.concatenate(pieces, 1))
+            grads = jnp.concatenate(blocks, 0)
+            at_ = slice(i * rb, (i + 1) * rb)
+            crawl_acc[at_, :] += jnp.dot(grads, some_bench, preferred_element_type=F32)
+            product = jnp.dot(crawl_t[:, at_], grads, preferred_element_type=F32)
+            acc = product if acc is None else acc + product
+        out[...] = acc
+
+    piece = part // nz
+    quarters = part // 128
+    per = nz // quarters
+
+    def quarter(t):
+        u = quarters - 1 - t
+        if quarters == 4:
+            u = u + lax.div(u, 2) * (1 - 2 * lax.rem(u, 2))
+        return lax.rem(lax.div(z, per) + u, quarters)
+
+    def pass_on(t):
+        q = quarter(t)
+        take(yrecv.at[t, pl.ds(0, YS - 1)], y_rs.at[t])
+        total = yrecv[t, 0]
+        for i in range(1, YS):
+            total = total + yrecv[t, i]
+        zpart[pl.ds(pl.multiple_of(q * 128, 128), 128), :] = total.T
+        for i in range(per):
+            o = q * per + i
+            src = zpart.at[pl.ds(pl.multiple_of(o * piece, piece), piece), :]
+
+            @pl.when(o != z)
+            def _(o=o, src=src):
+                send(src, zrecv.at[z], fz_ss, fz_rs, at(k, y, o))
+
+            @pl.when(o == z)
+            def _(o=o, src=src):
+                zrecv[z] = src[...]
+
+    def gradient_step(t, carry):
+        q = quarter(t)
+        grad_chunk(1 - k, q, bench_part.at[t])
+        send(bench_part.at[t], sib.at[t], sib_ss, sib_rs.at[t], sibling)
+        grad_chunk(k, q, ysend.at[t])
+        take(sib.at[t], sib_rs.at[t])
+        for o in range(YS):
+            s = slice(o * 128, (o + 1) * 128)
+            ysend[t, :, s] = ysend[t, :, s] + sib[t, :, s]
+
+            @pl.when(o != y)
+            def _(o=o, s=s):
+                send(ysend.at[t, :, s], yrecv.at[t, y], y_ss, y_rs.at[t], at(k, o, z))
+
+            @pl.when(o == y)
+            def _(o=o, s=s):
+                yrecv[t, y] = ysend[t, :, s]
+
+        @pl.when(t >= 2)
+        def _():
+            pass_on(t - 2)
+
+        return carry
+
+    lax.fori_loop(0, quarters, gradient_step, 0)
+
+    quarter_rows = rows // nx
+    mine_rows = pl.ds(pl.multiple_of(c * quarter_rows, quarter_rows), quarter_rows)
+    for p in x_peers:
+        there = pl.ds(pl.multiple_of(p[1] * quarter_rows, quarter_rows), quarter_rows)
+        send(crawl_acc.at[there, :], crawl_recv.at[c], cr_ss, cr_rs, p)
     crawl_recv[c] = crawl_acc[mine_rows, :]
 
-    others = yrecv.at[pl.ds(0, YS - 1)]
-    take(others, y_rs)
-    piece = part // nz
-    for j in range(part // 128):
-        s = slice(j * 128, (j + 1) * 128)
-        total = yrecv[0, :, s]
-        for i in range(1, YS):
-            total = total + yrecv[i, :, s]
-        zpart[s, :] = total.T
-    for d, (o, p) in enumerate(z_peers):
-        send(zpart.at[pl.ds(pl.multiple_of(o * piece, piece), piece), :], zrecv.at[z], fz_ss.at[d], fz_rs, p)
-    zrecv[z] = zpart[pl.ds(pl.multiple_of(z * piece, piece), piece), :]
+    for t in range(max(quarters - 2, 0), quarters):
+        pass_on(t)
 
     take(crawl_recv.at[pl.ds(0, nx - 1)], cr_rs)
     crawl_out[mine_rows, :] = summed(crawl_recv, nx)
-    for d, p in enumerate(x_peers):
-        send(crawl_out.at[mine_rows, :], crawl_out.at[mine_rows, :], ca_ss.at[d], ca_rs, p)
+    for p in x_peers:
+        send(crawl_out.at[mine_rows, :], crawl_out.at[mine_rows, :], ca_ss, ca_rs, p)
+
+    def place(y_, z_):
+        return bench_out.at[pl.ds(pl.multiple_of(k * half + y_ * part + z_ * piece, piece), piece), :]
+
+    def back(v, d, n):
+        return lax.rem(v + n - d, n)
 
     take(zrecv.at[pl.ds(0, nz - 1)], fz_rs)
-    block = pl.multiple_of(k * half + y * part, part)
-    own = pl.ds(pl.multiple_of(block + z * piece, piece), piece)
-    bench_out[own, :] = summed(zrecv, nz)
-    for d, (_, p) in enumerate(z_peers):
-        send(bench_out.at[own, :], bench_out.at[own, :], gz_ss.at[d], gz_rs, p)
-    take(zrecv.at[pl.ds(0, nz - 1)], gz_rs)
-    mine_block = pl.ds(block, part)
-    for s in range(YS - 1):
-        send(bench_out.at[mine_block, :], bench_out.at[mine_block, :], gy_ss.at[s], gy_rs.at[s], at(k, ordered(s), z))
-    send(bench_out.at[mine_block, :], bench_out.at[mine_block, :], gc_ss.at[YS - 1], gc_rs.at[YS - 1], sibling)
-    for s in range(YS - 1):
-        source = lax.rem(y + YS - (2, 1, 3)[s], YS)
-        theirs = pl.ds(pl.multiple_of(k * half + source * part, part), part)
-        take(bench_out.at[theirs, :], gy_rs.at[s])
-        send(bench_out.at[theirs, :], bench_out.at[theirs, :], gc_ss.at[s], gc_rs.at[s], sibling)
-    for s in range(YS):
-        take(sib.at[s], gc_rs.at[s])
-        take(sib.at[s], gc_ss.at[s])
-        take(sib.at[s], sib_ss.at[s])
-    for s in range(YS - 1):
-        take(sib.at[s], gy_ss.at[s])
-        take(sib.at[s], y_ss.at[s])
-    for d in range(nz - 1):
-        take(zrecv.at[0], fz_ss.at[d])
-        take(zrecv.at[0], gz_ss.at[d])
+    place(y, z)[...] = summed(zrecv, nz)
+    y_up, y_down = at(k, lax.rem(y + 1, YS), z), at(k, lax.rem(y + YS - 1, YS), z)
+    z_up, z_down = at(k, y, lax.rem(z + 1, nz)), at(k, y, lax.rem(z + nz - 1, nz))
+    ups = nz // 2
+
+    def forward(d):
+        got = place(y, back(z, d, nz))
+        if d:
+            take(got, gz_rs.at[d - 1])
+        if d < ups:
+            send(got, got, gz_ss, gz_rs.at[d], z_up)
+        if d == 0 and nz > 2 or d > ups + 1:
+            send(got, got, gz_ss, gz_rs.at[(d or nz) - 2], z_down)
+        send(got, got, gy_ss, gy_rs.at[0, d], y_up)
+        send(got, got, gy_ss, gy_rs.at[2, d], y_down)
+        send(got, got, gc_ss, gc_rs, sibling)
+
+    def relay(d):
+        for e, p, first in ((1, y_up, 0), (3, y_down, 1)):
+            y_, z_ = back(y, e, YS), back(z, d, nz)
+            got = place(y_, z_)
+            take(got, gy_rs.at[e - 1, d])
+            start_ = k * half + y_ * part + z_ * piece + first * (piece // 2)
+            some = bench_out.at[pl.ds(pl.multiple_of(start_, piece // 2), piece // 2), :]
+            send(some, some, gy_ss, gy_rs.at[1, d], p)
+            send(got, got, gc_ss, gc_rs, sibling)
+
+    def last(d):
+        got = place(back(y, 2, YS), back(z, d, nz))
+        take(got, gy_rs.at[1, d])
+        send(got, got, gc_ss, gc_rs, sibling)
+
+    order = sorted(range(nz), key=lambda d: min(d, nz - d))
+    lags = (3, 6)
+    for i in range(nz + lags[1]):
+        if i < nz:
+            forward(order[i])
+        if 0 <= i - lags[0] < nz:
+            relay(order[i - lags[0]])
+        if 0 <= i - lags[1] < nz:
+            last(order[i - lags[1]])
+
     take(crawl_recv.at[pl.ds(0, nx - 1)], ca_rs)
-    for d in range(nx - 1):
-        take(crawl_recv.at[0], ca_ss.at[d])
-        take(crawl_recv.at[0], cr_ss.at[d])
+    take(crawl_recv.at[pl.ds(0, nx - 1)], ca_ss)
+    take(crawl_recv.at[pl.ds(0, nx - 1)], cr_ss)
+    take(bench_out.at[pl.ds(0, half), :], gc_rs)
+    take(bench_out.at[pl.ds(0, half), :], gc_ss)
+    take(bench_out.at[pl.ds(0, half - part), :], gy_ss)
+    take(zrecv.at[pl.ds(0, nz - 1)], gz_ss)
+    take(zrecv.at[pl.ds(0, nz - 1)], fz_ss)
+    take(yrecv.at[:, pl.ds(0, YS - 1)], y_ss)
+    take(sib, sib_ss)
 
 
 def solution(mesh):
@@ -390,8 +446,6 @@
         scratch = [
             vmem((rows, cols), F32),
             vmem((depth, rows), jnp.bfloat16),
-            vmem((rows, part), jnp.bfloat16),
-            vmem((rows, 128), F32),
             vmem((rows, 128), F32),
             vmem((rows, 128), F32),
             vmem((rows, 128), F32),
@@ -406,13 +460,13 @@
             vmem((2, 1, half), F32), vmem((2, nz, 1, half), F32),
             vmem((3, CORES, 1, half), F32),
             vmem((rows, depth), F32), vmem((nx, rows // nx, depth), F32),
-            vmem((YS, depth, part), F32), vmem((YS, depth, part), F32),
-            vmem((YS, depth, part), F32), vmem((YS, depth, part), F32),
+            vmem((part // 128, depth, YS * 128), F32), vmem((part // 128, depth, YS * 128), F32),
+            vmem((part // 128, depth, YS * 128), F32), vmem((part // 128, YS, depth, 128), F32),
             vmem((part, depth), F32), vmem((nz, part // nz, depth), F32),
             dma((4,)), dma((4,)), dma((3,)), dma((3,)), dma((3,)), dma((3,)), dma((3,)), dma((3,)),
-            dma((nx - 1,)), dma, dma((nx - 1,)), dma,
-            dma((YS,)), dma((YS,)), dma((YS - 1,)), dma, dma((nz - 1,)), dma,
-            dma((nz - 1,)), dma, dma((YS - 1,)), dma((YS - 1,)), dma((YS,)), dma((YS,)),
+            dma, dma, dma, dma,
+            dma, dma((part // 128,)), dma, dma((part // 128,)), dma, dma,
+            dma, dma((nz - 1,)), dma, dma((YS - 1, nz)), dma, dma,
         ]
         return pl.pallas_call(
             functools.partial(kernel, nx, nz),

time: 133 us -> 120 us (0.902)
  Pallas kernels: 126 us -> 114 us
    pallas_call x1, Pallas kernels: 126 us -> 114 us  [per_device(): pl.pallas_call(functools.partial(kernel, nx, nz), out_shape=(jax.ShapeDty...]
where the time goes in v2:
time: 120 us
  Pallas kernels  114 us (95%)
  local copies, waits for them, and re-layouts  4.91 us (4%)
    pallas_call x1, Pallas kernels, per_device(): pl.pallas_call(functools.partial(kernel, nx, nz), out_shape=(jax.ShapeDty...  114 us
    unnamed x2, local copies, waits for them, and re-layouts  4.91 us

profile of v2, /device:TPU:1, one launch (start us, length us, event | category | flops | bytes accessed | tf_op | source)
XLA Modules:
  0.0 119.6 jit_solution(3637387760239381887)
XLA Ops:
  0.6 114.0 %shard_map.68 = (f32[1024,128]{1,0:T(8,128)}, f32[4096,128]{1,0:T(8,128)}) custom-call(bf16[1024,128]{1,0:T(8,128)(2,1)} %crawl.1, bf16[4096,128]{1,0:T(8,128)(2,1)} %bench.1, f32[1,4096]{1,0:T(1,128)} %bitcast.3, f32[1,1024]{1,0:T(1,128)} %bitcast.5, f32[1,4096]{1,0:T(1,128)} %bitcast.4), custom_call_target="tpu_custom_call" | custom-call | tf_op jit(solution)/shard_map/pallas_call | solution.py:471
  114.7 1.9 %copy.9 = f32[1024,128]{1,0:T(8,128)} copy(f32[1024,128]{1,0:T(8,128)} %get-tuple-element.4) | data formatting | bytes 1048576
  116.5 3.0 %copy.10 = f32[4096,128]{1,0:T(8,128)} copy(f32[4096,128]{1,0:T(8,128)} %get-tuple-element.5) | data formatting | bytes 4194304

commit v3 on v2

--- a/solution.py
+++ b/solution.py
@@ -17,10 +17,10 @@
 
 def kernel(
     nx, nz,
-    crawl, bench, start, row_cot, col_cot,
+    crawl_in, bench_in, start_in, row_cot_in, col_cot_in,
     crawl_out, bench_out,
-    tile, crawl_t, lane_max, alpha_b, beta_b, back_b,
-    rowvec, colmax, fvec, gvec, avec, bvec,
+    crawl, bench, start, row_cot, col_cot, in_s, tile, crawl_t, lane_max, alpha_b, beta_b, back_b,
+    kept, rowvec, colmax, fvec, gvec, avec, bvec,
     xs1, xr1, xs, xr, as1, ar1, as_, ar, zs1, zr1, zs, zr, cg,
     crawl_acc, crawl_recv, bench_part, sib, ysend, yrecv, zpart, zrecv,
     x_ss, x_rs, a_ss, a_rs, z_ss, z_rs, g_ss, g_rs,
@@ -46,6 +46,15 @@
     z_peers = [(lax.rem(z + d, nz), at(k, y, lax.rem(z + d, nz))) for d in range(1, nz)]
     sibling = at(1 - k, y, z)
 
+    loads = [
+        pltpu.make_async_copy(src, dst, in_s.at[i])
+        for i, (src, dst) in enumerate((
+            (crawl_in, crawl), (bench_in, bench), (start_in, start), (row_cot_in, row_cot), (col_cot_in, col_cot),
+        ))
+    ]
+    for load in loads:
+        load.start()
+
     barrier = pltpu.get_barrier_semaphore()
     everyone = x_peers + [p for _, p in a_peers] + [p for _, p in z_peers]
     for p in everyone:
@@ -59,13 +68,19 @@
     def take(ref, sem):
         pltpu.make_async_copy(ref, ref, sem).wait()
 
-    def x_exchange(n, src, recv):
-        recv[c] = src[...]
+    hr = rows // 2
+    halves = [slice(h * hr, (h + 1) * hr) for h in range(2)]
+
+    def x_send(n, h, src, recv):
+        s = halves[h]
+        recv[c, :, s] = src[:, s]
         for p in x_peers:
-            send(src, recv.at[c], x_ss.at[n], x_rs.at[n], p)
-        others = recv.at[pl.ds(0, nx - 1)]
-        take(others, x_rs.at[n])
-        take(others, x_ss.at[n])
+            send(src.at[:, s], recv.at[c, :, s], x_ss.at[n, h], x_rs.at[n, h], p)
+
+    def x_take(n, h, recv):
+        others = recv.at[pl.ds(0, nx - 1), :, halves[h]]
+        take(others, x_rs.at[n, h])
+        take(others, x_ss.at[n, h])
 
     def a_exchange(n, src, recv):
         recv[a] = src[k]
@@ -89,27 +104,30 @@
         take(cg.at[n, k], g_rs.at[n])
         take(cg.at[n, k], g_ss.at[n])
 
-    def summed(recv, n):
-        total = recv[0]
+    def summed(recv, n, s=slice(None)):
+        total = recv[0, :, s]
         for i in range(1, n):
-            total = total + recv[i]
+            total = total + recv[i, :, s]
         return total
 
-    def combined(recv, n):
-        top = recv[0, 0:1, :]
+    def combined(recv, n, s=slice(None)):
+        top = recv[0, 0:1, s]
         for i in range(1, n):
-            top = jnp.maximum(top, recv[i, 0:1, :])
-        total = recv[0, 1:2, :] * jnp.exp2(recv[0, 0:1, :] - top)
+            top = jnp.maximum(top, recv[i, 0:1, s])
+        total = recv[0, 1:2, s] * jnp.exp2(recv[0, 0:1, s] - top)
         for i in range(1, n):
-            total = total + recv[i, 1:2, :] * jnp.exp2(recv[i, 0:1, :] - top)
+            total = total + recv[i, 1:2, s] * jnp.exp2(recv[i, 0:1, s] - top)
         return top, total
 
-    def spread(vec, out):
-        for i in range(rows // 128):
+    def spread(vec, out, h):
+        for i in range(hr // 128):
             piece = vec[:, i * 128 : (i + 1) * 128]
-            out[i * 128 : (i + 1) * 128, :] = jnp.broadcast_to(piece, (128, 128)).T
-
-    def row_pass(d, out):
+            o = h * hr + i * 128
+            out[o : o + 128, :] = jnp.broadcast_to(piece, (128, 128)).T
+
+    def row_pass(d, n):
+        out = xs.at[n]
+
         def step(i, carry):
             base = pl.multiple_of(i * 128, 128)
             pieces = []
@@ -123,28 +141,39 @@
             out[0:1, pl.ds(base, 128)] = jnp.sum(acc, 0, keepdims=True)
             return carry
 
-        lax.fori_loop(0, rows // 128, step, 0)
+        for h in range(2):
+            lax.fori_loop(h * (hr // 128), (h + 1) * (hr // 128), step, 0)
+            x_send(n + 1, h, out, xr.at[n])
 
     width = min(1024, cols)
 
-    def col_pass(w, finish):
+    def col_loop(h, init, step, keep, finish):
         for cb in range(cols // width):
-            def step(i, accs, cb=cb):
-                base = pl.multiple_of(i * 64, 64)
-                wb = w[pl.ds(base, 64), :]
-                new = []
-                for j in range(width // 128):
-                    o = cb * width + j * 128
-                    t = tile[pl.ds(base, 64), o : o + 128] * wb
-                    new.append(accs[j] + jnp.sum(t.reshape(8, 8, 128), 0))
-                return tuple(new)
-
-            accs = lax.fori_loop(
-                0, rows // 64, step, tuple(jnp.zeros((8, 128), F32) for _ in range(width // 128))
+            at_ = [slice(cb * width + j * 128, cb * width + (j + 1) * 128) for j in range(width // 128)]
+            first = tuple(jnp.full((8, 128), init, F32) if h == 0 else keep[:, s] for s in at_)
+            last_ = lax.fori_loop(
+                h * (hr // 64), (h + 1) * (hr // 64), lambda i, accs, at_=at_: step(i, accs, at_), first
             )
-            for j in range(width // 128):
-                finish(cb * width + j * 128, jnp.sum(accs[j], 0, keepdims=True))
-
+            for s, acc in zip(at_, last_):
+                if h == 0:
+                    keep[:, s] = acc
+                else:
+                    finish(s, acc)
+
+    def col_pass(w, ready, finish):
+        def step(i, accs, at_):
+            base = pl.multiple_of(i * 64, 64)
+            wb = w[pl.ds(base, 64), :]
+            return tuple(
+                acc + jnp.sum((tile[pl.ds(base, 64), s] * wb).reshape(8, 8, 128), 0) for acc, s in zip(accs, at_)
+            )
+
+        for h in range(2):
+            ready(h)
+            col_loop(h, 0.0, step, kept, lambda s, acc: finish(s.start, jnp.sum(acc, 0, keepdims=True)))
+
+    for load in loads:
+        load.wait()
     crawl_t[...] = crawl[...].astype(F32).T.astype(jnp.bfloat16)
     lane_max[...] = jnp.full(lane_max.shape, -jnp.inf, F32)
     mm = min(512, cols)
@@ -186,30 +215,30 @@
         xs1[1:2, pl.ds(base, 128)] = jnp.sum(acc * jnp.exp2(top - best), 0, keepdims=True)
         return carry
 
-    lax.fori_loop(0, rows // 128, level_step, 0)
-    pl.semaphore_wait(barrier, len(everyone))
-    x_exchange(0, xs1, xr1)
-    top, total = combined(xr1, nx)
-    spread(top + jnp.log2(total), alpha_b)
+    for h in range(2):
+        lax.fori_loop(h * (hr // 128), (h + 1) * (hr // 128), level_step, 0)
+        if h == 0:
+            pl.semaphore_wait(barrier, len(everyone))
+        x_send(0, h, xs1, xr1)
+
+    def top_step(i, tops, at_):
+        base = pl.multiple_of(i * 64, 64)
+        lev = alpha_b[pl.ds(base, 64), :]
+        return tuple(
+            jnp.maximum(top, jnp.max((tile[pl.ds(base, 64), s] - lev).reshape(8, 8, 128), 0))
+            for top, s in zip(tops, at_)
+        )
+
+    def top_finish(s, top):
+        colmax[0:1, s] = jnp.max(top, 0, keepdims=True)
+
+    for h in range(2):
+        x_take(0, h, xr1)
+        top, total = combined(xr1, nx, halves[h])
+        spread(top + jnp.log2(total), alpha_b, h)
+        col_loop(h, -jnp.inf, top_step, kept, top_finish)
 
     for cb in range(cols // width):
-        def top_step(i, tops, cb=cb):
-            base = pl.multiple_of(i * 64, 64)
-            lev = alpha_b[pl.ds(base, 64), :]
-            new = []
-            for j in range(width // 128):
-                o = cb * width + j * 128
-                t = tile[pl.ds(base, 64), o : o + 128] - lev
-                new.append(jnp.maximum(tops[j], jnp.max(t.reshape(8, 8, 128), 0)))
-            return tuple(new)
-
-        tops = lax.fori_loop(
-            0, rows // 64, top_step, tuple(jnp.full((8, 128), -jnp.inf, F32) for _ in range(width // 128))
-        )
-        tops = [jnp.max(t, 0, keepdims=True) for t in tops]
-        for j in range(width // 128):
-            colmax[0:1, cb * width + j * 128 : cb * width + (j + 1) * 128] = tops[j]
-
         def exp_step(i, accs, cb=cb):
             base = pl.multiple_of(i * 64, 64)
             lev = alpha_b[pl.ds(base, 64), :]
@@ -227,7 +256,7 @@
         for j in range(width // 128):
             o = cb * width + j * 128
             h, p = o // half, o % half
-            as1[h, 0:1, p : p + 128] = tops[j]
+            as1[h, 0:1, p : p + 128] = colmax[0:1, o : o + 128]
             as1[h, 1:2, p : p + 128] = jnp.sum(accs[j], 0, keepdims=True)
     gvec[...] = jnp.exp2(colmax[...])
 
@@ -242,41 +271,47 @@
         s = slice(h * half, (h + 1) * half)
         fvec[0:1, s] = jnp.exp2(colmax[0:1, s] - cg[0, h])
 
-    row_pass(fvec, xs.at[0])
-    x_exchange(1, xs.at[0], xr.at[0])
-    alpha = 1.0 / summed(xr.at[0], nx)
-    rowvec[...] = alpha
-    spread(alpha, alpha_b)
-
-    def col_reduce(n, w):
+    row_pass(fvec, 0)
+
+    def alpha_ready(h):
+        x_take(1, h, xr.at[0])
+        alpha = 1.0 / summed(xr.at[0], nx, halves[h])
+        rowvec[:, halves[h]] = alpha
+        spread(alpha, alpha_b, h)
+
+    def col_reduce(n, w, ready):
         def finish(o, v):
             h, p = o // half, o % half
             as_[n, h, 0:1, p : p + 128] = v * fvec[0:1, o : o + 128]
 
-        col_pass(w, finish)
+        col_pass(w, ready, finish)
         a_exchange(n + 1, as_.at[n], ar.at[n])
         zs[n] = summed(ar.at[n], na)
         z_exchange(n + 1, zs.at[n], zr.at[n])
         core_gather(n + 1, summed(zr.at[n], nz))
 
-    col_reduce(0, alpha_b)
+    col_reduce(0, alpha_b, alpha_ready)
     for h in range(CORES):
         s = slice(h * half, (h + 1) * half)
         avec[0:1, s] = fvec[0:1, s] * col_cot[0:1, s] / cg[1, h]
 
-    row_pass(avec, xs.at[1])
-    x_exchange(2, xs.at[1], xr.at[1])
-    back2 = row_cot[...] - rowvec[...] * summed(xr.at[1], nx)
-    spread(back2 * rowvec[...], beta_b)
-
-    col_reduce(1, beta_b)
+    row_pass(avec, 1)
+
+    def beta_ready(h):
+        x_take(2, h, xr.at[1])
+        alpha = rowvec[:, halves[h]]
+        back2 = row_cot[:, halves[h]] - alpha * summed(xr.at[1], nx, halves[h])
+        spread(back2 * alpha, beta_b, h)
+
+    col_reduce(1, beta_b, beta_ready)
     for h in range(CORES):
         s = slice(h * half, (h + 1) * half)
         bvec[0:1, s] = -fvec[0:1, s] * cg[2, h]
 
-    row_pass(bvec, xs.at[2])
-    x_exchange(3, xs.at[2], xr.at[2])
-    spread(-summed(xr.at[2], nx), back_b)
+    row_pass(bvec, 2)
+    for h in range(2):
+        x_take(3, h, xr.at[2])
+        spread(-summed(xr.at[2], nx, halves[h]), back_b, h)
 
     crawl_acc[...] = jnp.zeros(crawl_acc.shape, F32)
 
@@ -444,13 +479,15 @@
         half, part = cols // CORES, cols // (CORES * YS)
         vmem, dma = pltpu.VMEM, pltpu.SemaphoreType.DMA
         scratch = [
+            vmem((rows, depth), jnp.bfloat16), vmem((cols, depth), jnp.bfloat16),
+            vmem((1, cols), F32), vmem((1, rows), F32), vmem((1, cols), F32), dma((5,)),
             vmem((rows, cols), F32),
             vmem((depth, rows), jnp.bfloat16),
             vmem((rows, 128), F32),
             vmem((rows, 128), F32),
             vmem((rows, 128), F32),
             vmem((rows, 128), F32),
-            vmem((1, rows), F32),
+            vmem((8, cols), F32), vmem((1, rows), F32),
             *[vmem((1, cols), F32)] * 5,
             vmem((2, rows), F32), vmem((nx, 2, rows), F32),
             vmem((3, 1, rows), F32), vmem((3, nx, 1, rows), F32),
@@ -463,15 +500,15 @@
             vmem((part // 128, depth, YS * 128), F32), vmem((part // 128, depth, YS * 128), F32),
             vmem((part // 128, depth, YS * 128), F32), vmem((part // 128, YS, depth, 128), F32),
             vmem((part, depth), F32), vmem((nz, part // nz, depth), F32),
-            dma((4,)), dma((4,)), dma((3,)), dma((3,)), dma((3,)), dma((3,)), dma((3,)), dma((3,)),
+            dma((4, 2)), dma((4, 2)), dma((3,)), dma((3,)), dma((3,)), dma((3,)), dma((3,)), dma((3,)),
             dma, dma, dma, dma,
             dma, dma((part // 128,)), dma, dma((part // 128,)), dma, dma,
             dma, dma((nz - 1,)), dma, dma((YS - 1, nz)), dma, dma,
         ]
         return pl.pallas_call(
             functools.partial(kernel, nx, nz),
-            out_shape=(jax.ShapeDtypeStruct((rows, depth), F32), jax.ShapeDtypeStruct((cols, depth), F32)),
-            in_specs=[pl.BlockSpec(memory_space=vmem)] * 5,
+            out_shape=(vmem((rows, depth), F32), vmem((cols, depth), F32)),
+            in_specs=[pl.BlockSpec(memory_space=pltpu.HBM)] * 5,
             out_specs=(pl.BlockSpec(memory_space=vmem),) * 2,
             scratch_shapes=scratch,
             compiler_params=pltpu.CompilerParams(

time: 120 us -> 113 us (0.942)
  Pallas kernels: 114 us -> 110 us
  local copies, waits for them, and re-layouts: 4.91 us -> 2.11 us
    pallas_call x1, Pallas kernels: 114 us -> 110 us  [per_device(): pl.pallas_call(functools.partial(kernel, nx, nz), out_shape=(vmem((rows,...]
    unnamed x2, local copies, waits for them, and re-layouts: 4.91 us -> 2.11 us
where the time goes in v3:
time: 113 us
  Pallas kernels  110 us (97%)
  local copies, waits for them, and re-layouts  2.11 us (2%)
    pallas_call x1, Pallas kernels, per_device(): pl.pallas_call(functools.partial(kernel, nx, nz), out_shape=(vmem((rows,...  110 us

profile of v3, /device:TPU:1, one launch (start us, length us, event | category | flops | bytes accessed | tf_op | source)
XLA Modules:
  0.0 112.9 jit_solution(8502387699621947609)
XLA Ops:
  0.6 110.2 %shard_map.68 = (f32[1024,128]{1,0:T(8,128)S(1)}, f32[4096,128]{1,0:T(8,128)S(1)}) custom-call(bf16[1024,128]{1,0:T(8,128)(2,1)} %crawl_in.1, bf16[4096,128]{1,0:T(8,128)(2,1)} %bench_in.1, f32[1,4096]{1,0:T(1,128)} %bitcast.3, f32[1,1024]{1,0:T(1,128)} %bitcast.5, f32[1,4096]{1,0:T(1,128)} %bitcast.4), custom_call_target="tpu_custom_call" | custom-call | tf_op jit(solution)/shard_map/pallas_call | solution.py:508
  110.8 0.8 copy.9
  111.6 1.3 %copy.10 = f32[4096,128]{1,0:T(8,128)} copy(f32[4096,128]{1,0:T(8,128)S(1)} %get-tuple-element.3) | data formatting | bytes 4194304

commit v4 on v3

--- a/solution.py
+++ b/solution.py
@@ -38,12 +38,13 @@
     def at(k_, y_, z_):
         return ((z_ * YS + y_) * CORES + k_, c)
 
-    x_peers = [(r, lax.rem(c + d, nx)) for d in range(1, nx)]
+    x_peers = [(r, lax.rem(c + d, nx)) for d in sorted(range(1, nx), key=lambda d: -min(d, nx - d))]
     a_peers = []
-    for d in range(1, na):
+    for d in (4, 5, 3, 2, 6, 7, 1):
         o = lax.rem(a + d, na)
         a_peers.append((lax.rem(o, CORES), at(lax.rem(o, CORES), lax.div(o, CORES), z)))
-    z_peers = [(lax.rem(z + d, nz), at(k, y, lax.rem(z + d, nz))) for d in range(1, nz)]
+    by_far = sorted(range(1, nz), key=lambda d: -min(d, nz - d))
+    z_peers = [(lax.rem(z + d, nz), at(k, y, lax.rem(z + d, nz))) for d in by_far]
     sibling = at(1 - k, y, z)
 
     loads = [
@@ -142,7 +143,7 @@
             return carry
 
         for h in range(2):
-            lax.fori_loop(h * (hr // 128), (h + 1) * (hr // 128), step, 0)
+            lax.fori_loop(h * (hr // 128), (h + 1) * (hr // 128), step, 0, unroll=2)
             x_send(n + 1, h, out, xr.at[n])
 
     width = min(1024, cols)
@@ -152,7 +153,7 @@
             at_ = [slice(cb * width + j * 128, cb * width + (j + 1) * 128) for j in range(width // 128)]
             first = tuple(jnp.full((8, 128), init, F32) if h == 0 else keep[:, s] for s in at_)
             last_ = lax.fori_loop(
-                h * (hr // 64), (h + 1) * (hr // 64), lambda i, accs, at_=at_: step(i, accs, at_), first
+                h * (hr // 64), (h + 1) * (hr // 64), lambda i, accs, at_=at_: step(i, accs, at_), first, unroll=2
             )
             for s, acc in zip(at_, last_):
                 if h == 0:
@@ -195,7 +196,7 @@
         lane_max[pl.ds(base, rb), :] = top
         return carry
 
-    lax.fori_loop(0, (rows // rb) * (cols // mm), score_step, 0, unroll=4)
+    lax.fori_loop(0, (rows // rb) * (cols // mm), score_step, 0, unroll=8)
 
     def level_step(i, carry):
         base = pl.multiple_of(i * 128, 128)
@@ -427,6 +428,7 @@
             send(got, got, gz_ss, gz_rs.at[d], z_up)
         if d == 0 and nz > 2 or d > ups + 1:
             send(got, got, gz_ss, gz_rs.at[(d or nz) - 2], z_down)
+        send(got, got, gy_ss, gy_rs.at[1, d], at(k, lax.rem(y + 2, YS), z))
         send(got, got, gy_ss, gy_rs.at[0, d], y_up)
         send(got, got, gy_ss, gy_rs.at[2, d], y_down)
         send(got, got, gc_ss, gc_rs, sibling)
@@ -436,9 +438,6 @@
             y_, z_ = back(y, e, YS), back(z, d, nz)
             got = place(y_, z_)
             take(got, gy_rs.at[e - 1, d])
-            start_ = k * half + y_ * part + z_ * piece + first * (piece // 2)
-            some = bench_out.at[pl.ds(pl.multiple_of(start_, piece // 2), piece // 2), :]
-            send(some, some, gy_ss, gy_rs.at[1, d], p)
             send(got, got, gc_ss, gc_rs, sibling)
 
     def last(d):

time: 113 us -> 107 us (0.947)
  Pallas kernels: 110 us -> 104 us
    pallas_call x1, Pallas kernels: 110 us -> 104 us  [per_device(): pl.pallas_call(functools.partial(kernel, nx, nz), out_shape=(vmem((rows,...]
where the time goes in v4:
time: 107 us
  Pallas kernels  104 us (97%)
  local copies, waits for them, and re-layouts  2.11 us (2%)
    pallas_call x1, Pallas kernels, per_device(): pl.pallas_call(functools.partial(kernel, nx, nz), out_shape=(vmem((rows,...  104 us

profile of v4, /device:TPU:1, one launch (start us, length us, event | category | flops | bytes accessed | tf_op | source)
XLA Modules:
  0.0 107.2 jit_solution(13381743202184693277)
XLA Ops:
  0.6 104.4 %shard_map.68 = (f32[1024,128]{1,0:T(8,128)S(1)}, f32[4096,128]{1,0:T(8,128)S(1)}) custom-call(bf16[1024,128]{1,0:T(8,128)(2,1)} %crawl_in.1, bf16[4096,128]{1,0:T(8,128)(2,1)} %bench_in.1, f32[1,4096]{1,0:T(1,128)} %bitcast.3, f32[1,1024]{1,0:T(1,128)} %bitcast.5, f32[1,4096]{1,0:T(1,128)} %bitcast.4), custom_call_target="tpu_custom_call" | custom-call | tf_op jit(solution)/shard_map/pallas_call | solution.py:507
  105.1 0.8 copy.9
  105.9 1.3 %copy.10 = f32[4096,128]{1,0:T(8,128)} copy(f32[4096,128]{1,0:T(8,128)S(1)} %get-tuple-element.3) | data formatting | bytes 4194304

commit v5 on v4

--- a/solution.py
+++ b/solution.py
@@ -74,9 +74,9 @@
 
     def x_send(n, h, src, recv):
         s = halves[h]
-        recv[c, :, s] = src[:, s]
         for p in x_peers:
             send(src.at[:, s], recv.at[c, :, s], x_ss.at[n, h], x_rs.at[n, h], p)
+        recv[c, :, s] = src[:, s]
 
     def x_take(n, h, recv):
         others = recv.at[pl.ds(0, nx - 1), :, halves[h]]
@@ -84,17 +84,17 @@
         take(others, x_ss.at[n, h])
 
     def a_exchange(n, src, recv):
-        recv[a] = src[k]
         for o, p in a_peers:
             send(src.at[o], recv.at[a], a_ss.at[n], a_rs.at[n], p)
+        recv[a] = src[k]
         others = recv.at[pl.ds(0, na - 1)]
         take(others, a_rs.at[n])
         take(others, a_ss.at[n])
 
     def z_exchange(n, src, recv):
-        recv[z] = src[...]
         for _, p in z_peers:
             send(src, recv.at[z], z_ss.at[n], z_rs.at[n], p)
+        recv[z] = src[...]
         others = recv.at[pl.ds(0, nz - 1)]
         take(others, z_rs.at[n])
         take(others, z_ss.at[n])

time: 107 us -> 107 us (level)
  no operation moved by 1% of the time
where the time goes in v5:
time: 107 us
  Pallas kernels  104 us (97%)
  local copies, waits for them, and re-layouts  2.11 us (2%)
    pallas_call x1, Pallas kernels, per_device(): pl.pallas_call(functools.partial(kernel, nx, nz), out_shape=(vmem((rows,...  104 us

profile of v5, /device:TPU:1, one launch (start us, length us, event | category | flops | bytes accessed | tf_op | source)
XLA Modules:
  0.0 107.1 jit_solution(18213958458038785401)
XLA Ops:
  0.6 104.4 %shard_map.68 = (f32[1024,128]{1,0:T(8,128)S(1)}, f32[4096,128]{1,0:T(8,128)S(1)}) custom-call(bf16[1024,128]{1,0:T(8,128)(2,1)} %crawl_in.1, bf16[4096,128]{1,0:T(8,128)(2,1)} %bench_in.1, f32[1,4096]{1,0:T(1,128)} %bitcast.3, f32[1,1024]{1,0:T(1,128)} %bitcast.5, f32[1,4096]{1,0:T(1,128)} %bitcast.4), custom_call_target="tpu_custom_call" | custom-call | tf_op jit(solution)/shard_map/pallas_call | solution.py:507
  105.0 0.8 copy.9
  105.8 1.3 %copy.10 = f32[4096,128]{1,0:T(8,128)} copy(f32[4096,128]{1,0:T(8,128)S(1)} %get-tuple-element.3) | data formatting | bytes 4194304
